TPU v7x, 256 devices: a whole 4x4x8 slice. The times are simulated.
256 devices in a mesh: body: 8 (over x, core), cont: 32 (over z, y).
Axes of the slice: x: 4, y: 4, z: 8, core: 2. Of those that a mesh axis runs over, the one named last changes fastest.
Arguments:
- jacobian: bfloat16 [8, 960, 3, 64, 384], P('body', 'cont'), may hold values from -0.1875 to 0.1875
- contact_block_row: int32 [8, 960], P('body', 'cont'), may hold values from 0 to 79
- block_col: int32 [8, 960], P('body', 'cont'), may hold values from 0 to 159, as said below
- live_count: int32 [32, 80], P('cont', 'body'), may hold values from 1 to 64, as said below
- warm_start: float32 [3, 32, 5120], P(None, 'cont', 'body'), may hold values from -3 to 3
- step_size: float32 [3, 32, 5120], P(None, 'cont', 'body'), may hold values from 0.04 to 0.2
- bias: float32 [32, 5120], P('cont', 'body'), may hold values from -6 to 6
- friction: float32 [32, 5120], P('cont', 'body'), may hold values from 0.2 to 0.9
- free_velocity: float32 [8, 160, 384], P('body', 'cont'), may hold values from -6 to 6
- inv_mass: float32 [8, 160, 384], P('body', 'cont'), may hold values from 0.25 to 2
Outputs:
- impulse: float32 [3, 32, 5120], P(None, 'cont', 'body')
- velocity: float32 [8, 160, 384], P('body', 'cont')
Inputs may be any that keep to these rules, and one draw needn't show every extreme that they name: `block_col`: of the 30 blocks of one device (fixed b, q // 30 fixed), at most 3 name body blocks whose index // 5 is the same owner; in each body group one owner is named by exactly 3 blocks of every device of the group. `live_count`: the counts of contact group c are drawn evenly between 1 + (31 - c) * 63 // 31 and 64, so every block of contact group 0 has all 64 contacts live.
All inputs are finite; a program needn't handle non-finite values.
Results may differ from a plain program's by a relative error of at most 0.002.
Values may be sent and summed in bfloat16 or wider, within the bound.
A program may use at most 64 MiB of HBM per device.

v0:
```python
import jax
import jax.numpy as jnp
from jax import lax
from jax.sharding import PartitionSpec as P

SWEEPS = 3


exact_mode = lax.Precision.HIGHEST


def cone_update(present_impulse, local_velocity, step_now, shift_now, friction_now, active_now):
    trial_step = present_impulse - step_now * (local_velocity + shift_now)
    normal = jnp.maximum(trial_step[0], 0.0)
    cone_limit = friction_now * normal
    tangent = jnp.clip(trial_step[1:], -cone_limit, cone_limit)
    return jnp.concatenate([normal[None], tangent], axis=0) * active_now


def stacked_shift(bias_now):
    zero_part = jnp.zeros_like(bias_now)
    return jnp.stack([bias_now, zero_part, zero_part])


def shards(
    jacobian,
    contact_block_row,
    block_col,
    live_count,
    warm_start,
    step_size,
    bias,
    friction,
    free_velocity,
    inv_mass,
):
    blocks = jacobian[0]
    row_ids = contact_block_row[0]
    col_ids = block_col[0]
    slot_count = row_ids.shape[0]
    per_block = blocks.shape[2]
    owned_bodies = free_velocity.shape[1]
    owned_contacts = live_count.shape[1]
    cont_size = lax.axis_size("cont")
    body_size = lax.axis_size("body")
    group_bodies = owned_bodies * cont_size
    group_contacts = owned_contacts * body_size
    positions = lax.broadcasted_iota(jnp.int32, (owned_contacts, per_block), 1)
    active_mask = (
        (positions < live_count[0][:, None])
        .astype(jnp.float32)
        .reshape(1, owned_contacts * per_block)
    )
    row_onehot = (
        lax.broadcasted_iota(jnp.int32, (group_contacts, slot_count), 0) == row_ids[None, :]
    ).astype(jnp.float32)
    normal_shift = stacked_shift(bias)
    impulse_state = warm_start * active_mask

    def slot_impulses(current):
        rounded_result = lax.all_gather(current.astype(jnp.bfloat16), "body", axis=2, tiled=True)
        return jnp.take(rounded_result.reshape(3, group_contacts, per_block), row_ids, axis=1)

    col_onehot = (
        lax.broadcasted_iota(jnp.int32, (group_bodies, slot_count), 0) == col_ids[None, :]
    ).astype(jnp.float32)

    def settle(slot_force):
        force_sum = lax.psum_scatter(
            jnp.dot(col_onehot, slot_force, precision=exact_mode),
            "cont",
            scatter_dimension=0,
            tiled=True,
        )
        return free_velocity[0] + inv_mass[0] * force_sum

    for sweep_no in range(SWEEPS):
        slot_force = jnp.einsum(
            "sijd,isj->sd", blocks, slot_impulses(impulse_state), preferred_element_type=jnp.float32
        )
        velocity_state = settle(slot_force)
        group_rows = lax.all_gather(velocity_state.astype(jnp.bfloat16), "cont", axis=0, tiled=True)
        slot_local = jnp.einsum(
            "sijd,sd->isj",
            blocks,
            jnp.take(group_rows, col_ids, axis=0),
            preferred_element_type=jnp.float32,
        )
        summed_rows = jnp.einsum("gs,isj->igj", row_onehot, slot_local, precision=exact_mode)
        local_velocity = lax.psum_scatter(
            summed_rows.reshape(3, 1, group_contacts * per_block),
            "body",
            scatter_dimension=2,
            tiled=True,
        )
        impulse_state = cone_update(
            impulse_state, local_velocity, step_size, normal_shift, friction, active_mask
        )
    slot_force = jnp.einsum(
        "sijd,isj->sd", blocks, slot_impulses(impulse_state), preferred_element_type=jnp.float32
    )
    velocity_state = settle(slot_force)
    return (impulse_state, velocity_state[None])


def solution(mesh):
    placed = (
        P("body", "cont", None, None, None),
        P("body", "cont"),
        P("body", "cont"),
        P("cont", "body"),
        P(None, "cont", "body"),
        P(None, "cont", "body"),
        P("cont", "body"),
        P("cont", "body"),
        P("body", "cont", None),
        P("body", "cont", None),
    )
    return jax.shard_map(
        shards,
        mesh=mesh,
        in_specs=placed,
        out_specs=(P(None, "cont", "body"), P("body", "cont", None)),
        check_vma=False,
    )
```

profile of v0, /device:TPU:1, one launch (start us, length us, event | category | flops | bytes accessed | tf_op | source)
XLA Modules:
  0.0 937.4 jit_solution(12760455091539445436)
XLA Ops:
  7.3 0.7 compare_and_fusion.1
  7.9 0.7 compare_select_fusion.1
  8.6 0.7 fusion.62
  9.3 0.1 reshape.380
  9.4 0.7 fusion.58
  10.1 15.8 %all_gather.21 = bf16[3,1,5120]{2,0,1:T(4,128)(2,1)S(1)} all-gather(bf16[3,1,640]{2,0,1:T(4,128)(2,1)S(1)} %fusion.58), channel_id=1, replica_groups=mesh['body'=8,'cont'=32] {'body'}, dimensions={2}, use_global_device_ids=true | all-gather | bytes 34560 | tf_op jit(solution)/shard_map/all_gather | solution.py:61
  25.9 0.1 reshape.373
  26.1 0.6 gather_fusion
  26.7 0.1 select_bitcast_fusion.3
  26.8 3.2 fusion.12
  30.0 0.9 fusion.17
  31.1 0.6 dynamic-slice
  32.3 138.3 %all-reduce.10.cloned.1.call-done = f32[160,384]{1,0:T(8,128)} async-done(((f32[160,384]{1,0:T(8,128)}), f32[160,384]{1,0:T(8,128)}) %all-reduce.10.cloned.1.call-update) | async-done | bytes 245776
  170.7 0.7 fusion.67
  171.4 33.9 %all-gather = bf16[32,5,384]{2,1,0:T(8,128)(2,1)S(1)} all-gather(bf16[1,5,384]{2,1,0:T(8,128)(2,1)S(1)} %fusion.67), channel_id=1, replica_groups=mesh['body'=8,'cont'=32] {'cont'}, dimensions={0}, use_global_device_ids=true | all-gather | bytes 126720 | tf_op jit(solution)/shard_map/all_gather | solution.py:82
  205.4 0.6 gather_fusion.1
  206.0 0.1 select_bitcast_fusion.6
  206.1 4.4 fusion.10
  210.5 0.3 convolution_bitcast_fusion.2
  210.8 3.4 copy.59
  214.3 48.5 %reduce-scatter.10.cloned.1.call-done = f32[640,3]{1,0:T(8,128)} async-done(((f32[5120,3]{1,0:T(8,128)}), f32[640,3]{1,0:T(8,128)}) %reduce-scatter.10.cloned.1.call-update) | async-done | bytes 7696
  262.8 1.1 copy.54
  264.0 15.9 %all_gather.23 = bf16[3,1,5120]{2,0,1:T(4,128)(2,1)S(1)} all-gather(bf16[3,1,640]{2,0,1:T(4,128)(2,1)S(1)} %fusion.64), channel_id=1, replica_groups=mesh['body'=8,'cont'=32] {'body'}, dimensions={2}, use_global_device_ids=true | all-gather | bytes 34560 | tf_op jit(solution)/shard_map/all_gather | solution.py:61
  279.9 0.1 reshape.375
  280.1 0.6 gather_fusion.2
  280.7 0.1 select_bitcast_fusion.2
  280.8 3.2 fusion.8
  284.0 0.9 fusion.16
  285.0 138.5 %all-reduce.12.cloned.1.call-done = f32[160,384]{1,0:T(8,128)} async-done(((f32[160,384]{1,0:T(8,128)}), f32[160,384]{1,0:T(8,128)}) %all-reduce.12.cloned.1.call-update) | async-done | bytes 245776
  423.5 0.7 fusion.66
  424.2 33.9 %all-gather.1 = bf16[32,5,384]{2,1,0:T(8,128)(2,1)S(1)} all-gather(bf16[1,5,384]{2,1,0:T(8,128)(2,1)S(1)} %fusion.66), channel_id=1, replica_groups=mesh['body'=8,'cont'=32] {'cont'}, dimensions={0}, use_global_device_ids=true | all-gather | bytes 126720 | tf_op jit(solution)/shard_map/all_gather | solution.py:82
  458.2 0.6 gather_fusion.3
  458.8 0.1 select_bitcast_fusion.5
  458.9 4.4 fusion.6
  463.3 0.3 convolution_bitcast_fusion.1
  463.6 3.4 copy.60
  467.1 48.5 %reduce-scatter.12.cloned.1.call-done = f32[640,3]{1,0:T(8,128)} async-done(((f32[5120,3]{1,0:T(8,128)}), f32[640,3]{1,0:T(8,128)}) %reduce-scatter.12.cloned.1.call-update) | async-done | bytes 7696
  515.6 1.1 copy.56
  516.8 16.1 %all_gather.25 = bf16[3,1,5120]{2,0,1:T(4,128)(2,1)S(1)} all-gather(bf16[3,1,640]{2,0,1:T(4,128)(2,1)S(1)} %fusion.63), channel_id=1, replica_groups=mesh['body'=8,'cont'=32] {'body'}, dimensions={2}, use_global_device_ids=true | all-gather | bytes 34560 | tf_op jit(solution)/shard_map/all_gather | solution.py:61
  532.8 0.1 reshape.377
  533.0 0.6 gather_fusion.4
  533.6 0.1 select_bitcast_fusion.1
  533.7 3.2 fusion.4
  536.9 0.9 fusion.15
  537.9 138.5 %all-reduce.14.cloned.1.call-done = f32[160,384]{1,0:T(8,128)} async-done(((f32[160,384]{1,0:T(8,128)}), f32[160,384]{1,0:T(8,128)}) %all-reduce.14.cloned.1.call-update) | async-done | bytes 245776
  676.5 0.7 fusion.65
  677.2 33.9 %all-gather.2 = bf16[32,5,384]{2,1,0:T(8,128)(2,1)S(1)} all-gather(bf16[1,5,384]{2,1,0:T(8,128)(2,1)S(1)} %fusion.65), channel_id=1, replica_groups=mesh['body'=8,'cont'=32] {'cont'}, dimensions={0}, use_global_device_ids=true | all-gather | bytes 126720 | tf_op jit(solution)/shard_map/all_gather | solution.py:82
  711.1 0.6 gather_fusion.5
  711.7 0.1 select_bitcast_fusion.4
  711.8 4.4 fusion.2
  716.2 0.3 convolution_bitcast_fusion
  716.5 3.4 copy.61
  720.0 48.5 %reduce-scatter.14.cloned.1.call-done = f32[640,3]{1,0:T(8,128)} async-done(((f32[5120,3]{1,0:T(8,128)}), f32[640,3]{1,0:T(8,128)}) %reduce-scatter.14.cloned.1.call-update) | async-done | bytes 7696
  768.5 1.1 copy.58
  769.7 15.9 %all_gather.27 = bf16[3,1,5120]{2,0,1:T(4,128)(2,1)S(1)} all-gather(bf16[3,1,640]{2,0,1:T(4,128)(2,1)S(1)} %get-tuple-element.16), channel_id=1, replica_groups=mesh['body'=8,'cont'=32] {'body'}, dimensions={2}, use_global_device_ids=true | all-gather | bytes 34560 | tf_op jit(solution)/shard_map/all_gather | solution.py:61
  785.6 0.1 reshape.379
  785.8 0.6 gather_fusion.6
  786.4 0.1 select_bitcast_fusion
  786.5 3.2 fusion
  789.7 0.9 fusion.14
  790.7 0.6 copy.37
  791.3 137.9 %all-reduce.16.cloned.1.call-done = f32[160,384]{1,0:T(8,128)} async-done(((f32[160,384]{1,0:T(8,128)}), f32[160,384]{1,0:T(8,128)}) %all-reduce.16.cloned.1.call-update) | async-done | bytes 245776
  929.2 0.7 fusion.54
  929.9 0.6 copy.38
  (58 shorter events, 1.0 us)
Async XLA Ops:
  7.2 23.9 %copy-start.8 = (u32[256]{0:T(256)S(1)}, u32[256]{0:T(256)}, u32[]{:S(2)}) copy-start(u32[256]{0:T(256)} %constant.37) | copy-start | bytes 3076
  7.2 22.8 %copy-start.6 = (s32[1,30]{1,0:T(1,128)S(1)}, s32[1,30]{1,0:T(1,128)}, u32[]{:S(2)}) copy-start(s32[1,30]{1,0:T(1,128)} %param.16) | copy-start | bytes 364
  7.2 163.5 %copy-start = (f32[1,5,384]{2,0,1:T(1,128)S(1)}, f32[1,5,384]{2,0,1:T(1,128)}, u32[]{:S(2)}) copy-start(f32[1,5,384]{2,0,1:T(1,128)} %param.23) | copy-start | bytes 23044
  7.2 163.5 %copy-start.1 = (f32[1,5,384]{2,0,1:T(1,128)S(1)}, f32[1,5,384]{2,0,1:T(1,128)}, u32[]{:S(2)}) copy-start(f32[1,5,384]{2,0,1:T(1,128)} %param.22) | copy-start | bytes 23044
  7.2 163.5 %all-reduce.10.cloned.1.call-start = ((), (), s32[]{:S(2)}) async-start(), calls=%async_computation.6 | async-start | bytes 491520
  26.8 183.7 %copy-start.7 = (s32[1,30]{1,0:T(1,128)S(1)}, s32[1,30]{1,0:T(1,128)}, u32[]{:S(2)}) copy-start(s32[1,30]{1,0:T(1,128)} %param.15) | copy-start | bytes 364
  31.0 231.8 %reduce-scatter.10.cloned.1.call-start = ((), (), s32[]{:S(2)}) async-start(), calls=%async_computation.3 | async-start | bytes 2949120
  206.1 57.8 %copy-start.2 = (f32[3,1,640]{2,1,0:T(1,128)S(1)}, f32[3,1,640]{2,1,0:T(1,128)}, u32[]{:S(2)}) copy-start(f32[3,1,640]{2,1,0:T(1,128)} %param.19) | copy-start | bytes 23044
  206.1 57.8 %copy-start.3 = (f32[3,1,640]{2,1,0:T(1,128)S(1)}, f32[3,1,640]{2,1,0:T(1,128)}, u32[]{:S(2)}) copy-start(f32[3,1,640]{2,1,0:T(1,128)} %param.18) | copy-start | bytes 23044
  206.1 57.8 %copy-start.5 = (f32[1,640]{1,0:T(1,128)S(1)}, f32[1,640]{1,0:T(1,128)}, u32[]{:S(2)}) copy-start(f32[1,640]{1,0:T(1,128)} %param.20) | copy-start | bytes 7684
  206.1 57.9 %copy-start.4 = (f32[1,640]{1,0:T(1,128)S(1)}, f32[1,640]{1,0:T(1,128)}, u32[]{:S(2)}) copy-start(f32[1,640]{1,0:T(1,128)} %param.21) | copy-start | bytes 7684
  214.3 209.2 %all-reduce.12.cloned.1.call-start = ((), (), s32[]{:S(2)}) async-start(), calls=%async_computation.7 | async-start | bytes 491520
  285.0 230.6 %reduce-scatter.12.cloned.1.call-start = ((), (), s32[]{:S(2)}) async-start(), calls=%async_computation.4 | async-start | bytes 2949120
  467.0 209.4 %all-reduce.14.cloned.1.call-start = ((), (), s32[]{:S(2)}) async-start(), calls=%async_computation.8 | async-start | bytes 491520
  537.9 230.6 %reduce-scatter.14.cloned.1.call-start = ((), (), s32[]{:S(2)}) async-start(), calls=%async_computation.5 | async-start | bytes 2949120
  720.0 209.2 %all-reduce.16.cloned.1.call-start = ((), (), s32[]{:S(2)}) async-start(), calls=%async_computation.9 | async-start | bytes 491520
Sparse Core Ops, SparseCore 0:
  31.1 139.5 all-reduce.9
  214.4 48.3 reduce-scatter.9
  285.1 138.3 all-reduce.11
  467.1 48.3 reduce-scatter.11
  538.0 138.3 all-reduce.13
  720.1 48.3 reduce-scatter.13
  790.8 138.3 all-reduce.15
where the time goes:
time: 942 us; the launch traced here: 937 us
  waiting for transfers between devices  699 us (74%)
  blocking collectives  165 us (18%)
  matrix products  30.7 us (3%)
  local copies, waits for them, and re-layouts  20.6 us (2%)
  between operations  15.1 us (2%)
    unnamed x14, waiting for transfers between devices  699 us
    all_gather x3, blocking collectives, shards(): lax.all_gather(velocity_state.astype(jnp.bfloat16), 'cont', axis=0, tiled...  102 us
    all_gather x4, blocking collectives, slot_impulses(): lax.all_gather(current.astype(jnp.bfloat16), 'body', axis=2, tiled=True)  63.7 us
  transfers between devices with their start and end apart: 7, of which 7 were waited for; matrix products, arithmetic and copies ran while one was open for 0% of the time, Pallas kernels for 0%

commit v1 on v0

v1 whole, which is shorter than its diff:
```python
import jax
import jax.numpy as jnp
from jax import lax
from jax.experimental import pallas as pl
from jax.experimental.pallas import tpu as pltpu
from jax.sharding import PartitionSpec as P

MESH = pl.DeviceIdType.MESH
SWEEPS = 3
SLOTS = 30
F32, BF16, I32 = jnp.float32, jnp.bfloat16, jnp.int32


def iota(shape, dim):
    return lax.broadcasted_iota(I32, shape, dim)


def half_turn(x):
    return pltpu.roll(x, 64, axis=x.ndim - 1)


def split(x):
    hi = x.astype(BF16)
    mid = (x - hi.astype(F32)).astype(BF16)
    return hi, mid


def mm(a, b):
    return jnp.dot(a, b, preferred_element_type=F32)


def kernel(
    jac_in, row_in, col_in, live_in, warm_in, step_in, bias_in, fric_in, free_in, mass_in,
    imp_out, vel_out,
    jac, rowv, colv, livev, warm, step, bias, fric, free, mass,
    ids, pick, owner_one, slot_one, row_one, gather_one,
    imp_a, imp_b, free16, mass16,
    tab_send, tab_recv, con_send, con_recv, meta_send, meta_recv,
    force_send, force_recv, vel_send, vel_recv, loc_send, loc_recv,
    jac_sem, in_sem, tab_s, tab_r, con_s, con_r, meta_s, meta_r,
    force_s, force_r, vel_s, vel_r, loc_s, loc_r,
):
    b, c = lax.axis_index("body"), lax.axis_index("cont")
    x, core, z, y = b // 2, b % 2, c // 4, c % 4

    def cont_peer(k):
        i, j = k // 4, k % 4
        dz = 4 + (1 - 2 * (i % 2)) * ((i + 1) // 2)
        dy = 2 + (1 - 2 * (j % 2)) * ((j + 1) // 2)
        return ((z + dz) % 8) * 4 + (y + dy) % 4

    body_peers = [
        ((x + dx) % 4) * 2 + (core + dc) % 2
        for dx, dc in ((2, 1), (2, 0), (1, 1), (3, 1), (1, 0), (3, 0), (0, 1))
    ]

    def over_cont(go):
        def one(k, carry):
            go(cont_peer(k))
            return carry

        lax.fori_loop(0, 31, one, 0)

    def send_body(src, dst, ssem, rsem):
        for p in body_peers:
            pltpu.make_async_remote_copy(
                src_ref=src, dst_ref=dst, send_sem=ssem, recv_sem=rsem,
                device_id={"body": p}, device_id_type=MESH,
            ).start()

    def drain(ref, sem):
        pltpu.make_async_copy(ref, ref, sem).wait()

    bar = pltpu.get_barrier_semaphore()
    over_cont(lambda p: pl.semaphore_signal(bar, inc=1, device_id={"cont": p}, device_id_type=MESH))
    for p in body_peers:
        pl.semaphore_signal(bar, inc=1, device_id={"body": p}, device_id_type=MESH)

    pairs = (
        (row_in, rowv), (col_in, colv), (live_in, livev), (warm_in, warm), (step_in, step),
        (bias_in, bias), (fric_in, fric), (free_in, free), (mass_in, mass),
    )
    small = [pltpu.make_async_copy(s, d, in_sem.at[n]) for n, (s, d) in enumerate(pairs)]
    for cp in small:
        cp.start()
    blocks = [
        pltpu.make_async_copy(jac_in.at[pl.ds(n * 6, 6)], jac.at[pl.ds(n * 6, 6)], jac_sem.at[n])
        for n in range(5)
    ]
    for cp in blocks:
        cp.start()
    for cp in small:
        cp.wait()

    lane16 = iota((16, 128), 1)
    low16 = lane16 < 64
    lane8 = iota((8, 128), 1)
    low8 = lane8 < 64

    def rows_of(get):
        parts = [get(p).astype(F32) for p in range(5)]
        return jnp.concatenate(parts + [jnp.zeros((3, 128), F32)], axis=0)

    def planes(ref):
        w0, w1, w2 = [rows_of(lambda p, i=i: ref[i, 0:1, p * 128:(p + 1) * 128]) for i in range(3)]
        even = jnp.where(low8, w0, half_turn(w1))
        odd = jnp.where(low8, half_turn(w0), w1)
        return jnp.concatenate([even, odd], 0), jnp.concatenate([w2, half_turn(w2)], 0)

    def high_plane(ref):
        f = rows_of(lambda p: ref[0:1, p * 128:(p + 1) * 128])
        return jnp.concatenate([half_turn(f), f], 0)

    sub10 = iota((16, 10), 0)
    block_of_row = 2 * (sub10 & 7) + (sub10 >> 3)
    live_row = jnp.sum(
        jnp.where(iota((16, 10), 1) == block_of_row, livev[...].astype(F32), 0.0), axis=1, keepdims=True
    )
    active = (lane16 & 63).astype(F32) < live_row
    wa, wb = planes(warm)
    sa, sb = planes(step)
    tab_send[0] = jnp.where(active, wa, 0.0)
    tab_send[1] = jnp.where(low16, jnp.where(active, wb, 0.0), jnp.where(active, high_plane(fric), -1.0))
    con_send[0] = sa
    con_send[1] = jnp.where(low16, sb, high_plane(bias))

    ids[0:1, :] = jnp.where(iota((1, 128), 1) < 32, 9999, 0)
    ids[1:2, :] = jnp.where(iota((1, 128), 1) < 32, 10000, 0)
    ids[0:1, 0:SLOTS] = rowv[...]
    ids[1:2, 0:SLOTS] = colv[...]
    lane1 = iota((1, 128), 1)
    row_l = ids[0:1, :]
    dev = (row_l * 52429) >> 19
    kk = row_l - 10 * dev
    place_l = jnp.where(
        lane1 < SLOTS, dev * 16 + (kk & 1) * 8 + (kk >> 1), jnp.where(lane1 < 32, 9999, 0)
    ).astype(F32)
    col_l = ids[1:2, :]
    owner_i = (col_l * 52429) >> 18
    within_l = (col_l - 5 * owner_i).astype(F32)
    owner_l = owner_i.astype(F32)

    sub32, lane32 = iota((32, 128), 0), iota((32, 128), 1)

    def down(v):
        return jnp.sum(jnp.where(sub32 == lane32, jnp.broadcast_to(v, (32, 128)), 0.0), axis=1, keepdims=True)

    place_s, owner_s, within_s = down(place_l), down(owner_l), down(within_l)
    rank_l = jnp.sum(
        jnp.where((owner_s == owner_l) & (sub32 < lane32) & (lane32 < 32), 1.0, 0.0), axis=0, keepdims=True
    )
    con_send[2] = jnp.broadcast_to(pltpu.roll(jnp.broadcast_to(place_l, (8, 128)), (b % 4) * 32, axis=1)[0:1], (16, 128))

    def four_times(v):
        v = jnp.broadcast_to(v, (8, 128))
        v = v + pltpu.roll(v, 32, axis=1)
        return (v + pltpu.roll(v, 64, axis=1))[0:1]

    owner4, rank4 = four_times(owner_l), four_times(rank_l)
    sub = iota((288, 1), 0)
    o_row = jnp.where(sub < 256, sub >> 3, sub - 256)
    m_row = jnp.where(sub < 256, sub & 7, 8)
    r_row = jnp.where(m_row < 3, 0, jnp.where(m_row < 6, 1, 2))
    c_row = m_row - 3 * r_row
    hit = (owner4 == o_row.astype(F32)) & (rank4 == r_row.astype(F32))
    for tile in range(2):
        q = (iota((1, 128), 1) >> 5) + 4 * tile
        cq = jnp.where(q < 3, q, jnp.where(q < 6, q - 3, -1))
        pick[:, tile * 128:(tile + 1) * 128] = jnp.where(hit & (cq == c_row), 1.0, 0.0).astype(BF16)
    sub96 = iota((96, 1), 0)
    c96 = (sub96 >> 5).astype(F32)
    within96 = jnp.concatenate([within_s] * 3, axis=0)
    target96 = jnp.concatenate([owner_s * 16 + within_s] * 3, axis=0) + 5 * c96
    mark = jnp.where(iota((96, 128), 1).astype(F32) == within96 + 5 * c96, 1.0, 0.0).astype(BF16)
    mv = mm(pick[:, 0:96], mark)
    meta_send[:, 0:8, :] = mv[0:256].reshape(32, 8, 128)
    meta_send[:, 8:9, :] = mv[256:288].reshape(32, 1, 128)
    gather_one[...] = jnp.where(iota((96, 512), 1).astype(F32) == target96, 1.0, 0.0).astype(BF16)
    slot_one[...] = jnp.where(lane32.astype(F32) == place_s, 1.0, 0.0).astype(BF16)
    for src, dst in ((free, free16), (mass, mass16)):
        v = src[0]
        dst[...] = jnp.concatenate(
            [v[:, 0:128], v[:, 128:256], v[:, 256:384], jnp.zeros((1, 128), F32)], axis=0
        )

    pl.semaphore_wait(bar, 38)

    send_body(tab_send, tab_recv.at[b], tab_s, tab_r)
    tab_recv[b] = tab_send[...]
    send_body(con_send, con_recv.at[b], con_s, con_r)
    con_recv[b] = con_send[...]

    def send_meta(p):
        pltpu.make_async_remote_copy(
            src_ref=meta_send.at[p], dst_ref=meta_recv.at[c], send_sem=meta_s, recv_sem=meta_r,
            device_id={"cont": p}, device_id_type=MESH,
        ).start()

    over_cont(send_meta)
    meta_recv[c] = meta_send[c]

    drain(tab_recv.at[pl.ds(0, 7)], tab_r)
    imp_a[...] = tab_recv[:, 0].reshape(128, 128)
    imp_b[...] = tab_recv[:, 1].reshape(128, 128)
    for cp in blocks:
        cp.wait()

    low32 = lane32 < 64

    def forces():
        a, bb = imp_a[...].astype(BF16), imp_b[...].astype(BF16)
        ya, yb = mm(slot_one[...], a), mm(slot_one[...], bb)
        turned = half_turn(ya)
        pattern = jnp.concatenate(
            [ya, jnp.where(low32, yb, turned), jnp.where(low32, turned, half_turn(yb))], axis=1
        ).astype(BF16)
        halves = []
        row = iota((16, 768), 0)
        lane = iota((16, 768), 1) // 192
        for h in range(2):
            rep = jnp.concatenate([pattern[16 * h:16 * h + 16]] * 2, axis=1)
            acc = jnp.zeros((16, 384), F32)
            for g in range(0, 16, 4):
                s = 16 * h + g
                n = min(4, SLOTS - s)
                lhs = jnp.where(lane + g == row, rep, jnp.zeros_like(rep))[:, :n * 192]
                acc = acc + mm(lhs, jac[s:s + n].reshape(n * 192, 384))
            halves.append(acc)
        return jnp.concatenate(halves, axis=0)

    def locals_of(v):
        halves = []
        row = iota((16, 384), 0)
        lane = iota((16, 384), 1) // 192
        for h in range(2):
            acc = jnp.zeros((16, 384), F32)
            for g in range(0, 16, 4):
                s = 16 * h + g
                n = min(4, SLOTS - s)
                o = lax.dot_general(
                    v[16 * h:16 * h + 16], jac[s:s + n].reshape(n * 192, 384),
                    (((1,), (1,)), ((), ())), preferred_element_type=F32,
                )
                for p in range(0, n, 2):
                    acc = acc + jnp.where(lane + (g + p) == row, o[:, p * 192:p * 192 + 384], 0.0)
            halves.append(acc)
        return jnp.concatenate(halves, axis=0)

    def sweep(t, carry):
        hi, mid = split(forces())
        stacked = jnp.concatenate(
            [part[:, n * 128:(n + 1) * 128] for part in (hi, mid) for n in range(3)], axis=0
        )
        packed = mm(pick[:, 0:192], stacked)
        force_send[t, :, 0:8, :] = packed[0:256].reshape(32, 8, 128)
        force_send[t, :, 8:9, :] = packed[256:288].reshape(32, 1, 128)

        def send_force(p):
            pltpu.make_async_remote_copy(
                src_ref=force_send.at[t, p], dst_ref=force_recv.at[t, c], send_sem=force_s.at[t],
                recv_sem=force_r.at[t], device_id={"cont": p}, device_id_type=MESH,
            ).start()

        over_cont(send_force)
        force_recv[t, c] = force_send[t, c]

        @pl.when(t == 0)
        def _():
            drain(meta_recv.at[pl.ds(0, 31)], meta_r)
            meta = jnp.concatenate(
                [meta_recv[:, 0:8, :].reshape(256, 128), meta_recv[:, 8:9, :].reshape(32, 128),
                 jnp.zeros((96, 128), F32)], axis=0
            )
            owner_one[...] = jnp.transpose(meta)[0:16].astype(BF16)
            drain(con_recv.at[pl.ds(0, 7)], con_r)
            lo = con_recv[0, 2] + con_recv[1, 2] + con_recv[2, 2] + con_recv[3, 2]
            hi_ids = con_recv[4, 2] + con_recv[5, 2] + con_recv[6, 2] + con_recv[7, 2]
            sub128 = iota((128, 128), 0).astype(F32)
            row_one[:, 0:128] = jnp.where(sub128 == lo[0:1], 1.0, 0.0).astype(BF16)
            row_one[:, 128:256] = jnp.where(sub128 == hi_ids[0:1], 1.0, 0.0).astype(BF16)

        drain(force_recv.at[t, pl.ds(0, 31)], force_r.at[t])
        got = jnp.concatenate(
            [force_recv[t, :, 0:8, :].reshape(256, 128), force_recv[t, :, 8:9, :].reshape(32, 128),
             jnp.zeros((96, 128), F32)], axis=0
        )
        ghi, gmid = split(got)
        force = mm(owner_one[...], ghi) + mm(owner_one[...], gmid)
        velocity = free16[...] + mass16[...] * force

        @pl.when(t == SWEEPS)
        def _():
            for n in range(3):
                vel_out[0, :, n * 128:(n + 1) * 128] = velocity[n * 5:n * 5 + 5]

        @pl.when(t < SWEEPS)
        def _():
            vel_send[t] = velocity.astype(BF16)

            def send_vel(p):
                pltpu.make_async_remote_copy(
                    src_ref=vel_send.at[t], dst_ref=vel_recv.at[t, c], send_sem=vel_s.at[t],
                    recv_sem=vel_r.at[t], device_id={"cont": p}, device_id_type=MESH,
                ).start()

            over_cont(send_vel)
            vel_recv[t, c] = vel_send[t]
            drain(vel_recv.at[t, pl.ds(0, 31)], vel_r.at[t])
            vs = mm(gather_one[...], vel_recv[t].reshape(512, 128)).astype(BF16)
            v = jnp.concatenate([vs[0:32], vs[32:64], vs[64:96]], axis=1)
            loc = locals_of(v)
            l0, l1, l2 = loc[:, 0:128], loc[:, 128:256], loc[:, 256:384]
            even = (sub32 & 1) == 0
            t2 = half_turn(l2)
            la = jnp.where(even, l0, jnp.where(low32, half_turn(l1), t2))
            lb = jnp.where(even, l1, t2)
            ahi, amid = split(la)
            bhi = lb.astype(BF16).astype(F32)
            loc_send[t, 0] = ahi
            loc_send[t, 1] = amid
            loc_send[t, 2] = jnp.where(low32, bhi, half_turn(lb - bhi)).astype(BF16)
            send_body(loc_send.at[t], loc_recv.at[t, b], loc_s.at[t], loc_r.at[t])
            loc_recv[t, b] = loc_send[t]
            drain(loc_recv.at[t, pl.ds(0, 7)], loc_r.at[t])
            r1 = row_one[...]
            lva = mm(r1, loc_recv[t, :, 0].reshape(256, 128)) + mm(r1, loc_recv[t, :, 1].reshape(256, 128))
            lvb = mm(r1, loc_recv[t, :, 2].reshape(256, 128))
            lvb = lvb + half_turn(lvb)
            low = iota((128, 128), 1) < 64
            fric_high = tab_recv[:, 1].reshape(128, 128)
            step_b = con_recv[:, 1].reshape(128, 128)
            fr = jnp.where(low, half_turn(fric_high), fric_high)
            shift = jnp.where(low, half_turn(step_b), 0.0)
            ta = imp_a[...] - con_recv[:, 0].reshape(128, 128) * (lva + shift)
            tb = imp_b[...] - step_b * lvb
            normal = jnp.where(low, jnp.maximum(ta, 0.0), 0.0)
            lim_a = fr * half_turn(normal)
            lim_b = fr * normal
            live = fr >= 0.0
            new_a = jnp.where(low, normal, jnp.clip(ta, -lim_a, lim_a))
            imp_a[...] = jnp.where(live, new_a, 0.0)
            imp_b[...] = jnp.where(live & low, jnp.clip(tb, -lim_b, lim_b), 0.0)

        return carry

    lax.fori_loop(0, SWEEPS + 1, sweep, 0)

    own_a = imp_a[pl.ds(b * 16, 16), :]
    own_b = imp_b[pl.ds(b * 16, 16), :]
    ae, ao, be, bo = own_a[0:8], own_a[8:16], own_b[0:8], own_b[8:16]
    outs = (
        jnp.where(low8, ae, half_turn(ao)),
        jnp.where(low8, half_turn(ae), ao),
        jnp.where(low8, be, half_turn(bo)),
    )
    for i in range(3):
        for p in range(5):
            imp_out[i, 0:1, p * 128:(p + 1) * 128] = outs[i][p:p + 1]

    drain(tab_recv.at[pl.ds(0, 7)], tab_s)
    drain(con_recv.at[pl.ds(0, 7)], con_s)
    drain(meta_recv.at[pl.ds(0, 31)], meta_s)
    for t in range(SWEEPS + 1):
        drain(force_recv.at[t, pl.ds(0, 31)], force_s.at[t])
        if t < SWEEPS:
            drain(vel_recv.at[t, pl.ds(0, 31)], vel_s.at[t])
            drain(loc_recv.at[t, pl.ds(0, 7)], loc_s.at[t])


def shards(jacobian, row, col, live, warm, step, bias, fric, free, mass):
    dma = pltpu.SemaphoreType.DMA
    passes = SWEEPS + 1
    any_spec = pl.BlockSpec(memory_space=pl.ANY)
    vmem = pl.BlockSpec(memory_space=pltpu.VMEM)
    return pl.pallas_call(
        kernel,
        out_shape=(jax.ShapeDtypeStruct((3, 1, 640), F32), jax.ShapeDtypeStruct((1, 5, 384), F32)),
        in_specs=[any_spec] * 10,
        out_specs=(vmem, vmem),
        scratch_shapes=[
            pltpu.VMEM((SLOTS, 3, 64, 384), BF16),
            pltpu.VMEM((1, SLOTS), I32),
            pltpu.VMEM((1, SLOTS), I32),
            pltpu.VMEM((1, 10), I32),
            pltpu.VMEM((3, 1, 640), F32),
            pltpu.VMEM((3, 1, 640), F32),
            pltpu.VMEM((1, 640), F32),
            pltpu.VMEM((1, 640), F32),
            pltpu.VMEM((1, 5, 384), F32),
            pltpu.VMEM((1, 5, 384), F32),
            pltpu.VMEM((8, 128), I32),
            pltpu.VMEM((288, 256), BF16),
            pltpu.VMEM((16, 384), BF16),
            pltpu.VMEM((32, 128), BF16),
            pltpu.VMEM((128, 256), BF16),
            pltpu.VMEM((96, 512), BF16),
            pltpu.VMEM((128, 128), F32),
            pltpu.VMEM((128, 128), F32),
            pltpu.VMEM((16, 128), F32),
            pltpu.VMEM((16, 128), F32),
            pltpu.VMEM((2, 16, 128), F32),
            pltpu.VMEM((8, 2, 16, 128), F32),
            pltpu.VMEM((3, 16, 128), F32),
            pltpu.VMEM((8, 3, 16, 128), F32),
            pltpu.VMEM((32, 9, 128), F32),
            pltpu.VMEM((32, 9, 128), F32),
            pltpu.VMEM((passes, 32, 9, 128), F32),
            pltpu.VMEM((passes, 32, 9, 128), F32),
            pltpu.VMEM((SWEEPS, 16, 128), BF16),
            pltpu.VMEM((SWEEPS, 32, 16, 128), BF16),
            pltpu.VMEM((SWEEPS, 3, 32, 128), BF16),
            pltpu.VMEM((SWEEPS, 8, 3, 32, 128), BF16),
            dma((5,)), dma((9,)), dma, dma, dma, dma, dma, dma,
            dma((passes,)), dma((passes,)), dma((SWEEPS,)), dma((SWEEPS,)), dma((SWEEPS,)), dma((SWEEPS,)),
        ],
        compiler_params=pltpu.CompilerParams(
            collective_id=0, has_side_effects=True, vmem_limit_bytes=40 << 20
        ),
        name="sweeps",
    )(jacobian.reshape(jacobian.shape[1:]), row, col, live, warm, step, bias, fric, free, mass)


def solution(mesh):
    placed = (
        P("body", "cont", None, None, None),
        P("body", "cont"),
        P("body", "cont"),
        P("cont", "body"),
        P(None, "cont", "body"),
        P(None, "cont", "body"),
        P("cont", "body"),
        P("cont", "body"),
        P("body", "cont", None),
        P("body", "cont", None),
    )
    return jax.shard_map(
        shards,
        mesh=mesh,
        in_specs=placed,
        out_specs=(P(None, "cont", "body"), P("body", "cont", None)),
        check_vma=False,
    )
```

time: 942 us -> 92.5 us (0.10)
  waiting for transfers between devices: 699 us -> 0 us
  blocking collectives: 165 us -> 0 us
  Pallas kernels: 0 us -> 82 us
  matrix products: 30.7 us -> 0 us
  between operations: 15.1 us -> 0.65 us
  local copies, waits for them, and re-layouts: 20.6 us -> 9.56 us
    unnamed x14 -> x0, waiting for transfers between devices: 699 us -> none
    all_gather x7 -> x0, blocking collectives: 165 us -> none  [the longest x3 102 us: shards(): lax.all_gather(velocity_state.astype(jnp.bfloat16), 'cont', axis=0, tiled...]
    pallas_call x0 -> x1, Pallas kernels: none -> 82 us  [shards(): pl.pallas_call(kernel, out_shape=(jax.ShapeDtypeStruct((3, 1, 640), F32),...]
    dot_general x14 -> x0, matrix products: 30.7 us -> none  [the longest x3 13.1 us: shards(): jnp.einsum('sijd,sd->isj', blocks, jnp.take(group_rows, col_ids, axis=0),...]
  transfers between devices with their start and end apart: 7 -> 0, of which waited for: 7 -> 0; matrix products, arithmetic and copies ran while one was open for 0% -> 0% of each run, Pallas kernels for 0% -> 0%
where the time goes in v1:
time: 92.5 us; the launch traced here: 92.2 us
  Pallas kernels  82 us (89%)
  local copies, waits for them, and re-layouts  9.56 us (10%)
    pallas_call x1, Pallas kernels, shards(): pl.pallas_call(kernel, out_shape=(jax.ShapeDtypeStruct((3, 1, 640), F32),...  82 us
    unnamed x19, local copies, waits for them, and re-layouts  8.96 us

profile of v1, /device:TPU:1, one launch (start us, length us, event | category | flops | bytes accessed | tf_op | source)
XLA Modules:
  0.0 92.2 jit_solution(8290979419235435474)
XLA Ops:
  0.6 0.7 copy.12.free_in
  1.3 0.7 copy.13.mass_in
  2.0 0.0 copy-start
  2.0 2.3 %copy-done = bf16[1,30,3,64,384]{4,3,2,1,0:T(8,128)(2,1)S(1)} copy-done((bf16[1,30,3,64,384]{4,3,2,1,0:T(8,128)(2,1)S(1)}, bf16[1,30,3,64,384]{4,3,2,1,0:T(8,128)(2,1)}, u32[]{:S(2)}) %copy-start) | copy-done | bytes 4423704
  4.3 0.0 copy-start.1
  4.3 0.7 copy-done.1
  5.0 0.0 copy-start.2
  5.0 0.7 copy-done.2
  5.7 0.0 copy-start.3
  5.7 0.7 copy-done.3
  6.4 0.0 copy-start.4
  6.4 0.7 copy-done.4
  7.0 0.0 copy-start.5
  7.0 0.7 copy-done.5
  7.7 0.0 copy-start.6
  7.7 0.7 copy-done.6
  8.4 0.0 copy-start.7
  8.4 0.7 copy-done.7
  9.0 82.0 %sweeps.1 = (f32[3,1,640]{2,1,0:T(1,128)S(1)}, f32[1,5,384]{2,1,0:T(8,128)S(1)}) custom-call(bf16[30,3,64,384]{3,2,1,0:T(8,128)(2,1)S(1)} %bitcast.1, s32[1,30]{1,0:T(1,128)S(1)} %copy-done.5, s32[1,30]{1,0:T(1,128)S(1)} %copy-done.6, s32[1,10]{1,0:T(1,128)S(1)} %copy-done.7, f32[3,1,640]{2,1,0:T(1,128)S(1)} %copy-done.1, f32[3,1,640]{2,1,0:T(1,128)S(1)} %copy-done.2, ...), custom_call_target="tpu_custom_call" | custom-call | tf_op jit(solution)/shard_map/sweeps/pallas_call | solution.py:375
  91.0 0.6 copy.14
  91.6 0.6 copy.16
Async XLA Ops:
  2.0 2.3 %copy-start = (bf16[1,30,3,64,384]{4,3,2,1,0:T(8,128)(2,1)S(1)}, bf16[1,30,3,64,384]{4,3,2,1,0:T(8,128)(2,1)}, u32[]{:S(2)}) copy-start(bf16[1,30,3,64,384]{4,3,2,1,0:T(8,128)(2,1)} %param.10) | copy-start | bytes 13271044
  4.3 0.7 copy-start.1
  5.0 0.7 copy-start.2
  5.7 0.7 copy-start.3
  6.4 0.7 copy-start.4
  7.0 0.7 copy-start.5
  7.7 0.7 copy-start.6
  8.4 0.7 copy-start.7

commit v2 on v1

v2 whole, which is shorter than its diff:
```python
import jax
import jax.numpy as jnp
from jax import lax
from jax.experimental import pallas as pl
from jax.experimental.pallas import tpu as pltpu
from jax.sharding import PartitionSpec as P

MESH = pl.DeviceIdType.MESH
SWEEPS = 3
SLOTS = 30
NEAR = (
    (1, 2), (7, 2), (2, 1), (6, 1), (2, 0), (6, 0), (1, 1), (1, 3), (7, 1), (7, 3), (0, 2),
    (1, 0), (7, 0), (0, 1), (0, 3),
)
F32, BF16, I32 = jnp.float32, jnp.bfloat16, jnp.int32


def iota(shape, dim):
    return lax.broadcasted_iota(I32, shape, dim)


def half_turn(x):
    return pltpu.roll(x, 64, axis=x.ndim - 1)


def split(x):
    hi = x.astype(BF16)
    mid = (x - hi.astype(F32)).astype(BF16)
    return hi, mid


def mm(a, b):
    return jnp.dot(a, b, preferred_element_type=F32)


def kernel(
    jac_in, row_in, col_in, live_in, warm_in, step_in, bias_in, fric_in, free_in, mass_in,
    out,
    jac, rowv, colv, livev, warm, step, bias, fric, free, mass,
    jact, ids, pick, owner_one, slot_one, row_one, gather_one,
    imp_a, imp_b, step_a, step_b, fric48, shift48, home,
    tab_send, tab_recv, con_send, con_recv, meta_send, meta_recv,
    force_send, force_recv, vel_send, vel_recv, loc_send, loc_recv,
    jac_sem, in_sem, home_s, home_r, tab_s, tab_r, con_s, con_r, meta_s, meta_r,
    force_s, force_r, vel_s, vel_r, loc_s, loc_r,
):
    b, c = lax.axis_index("body"), lax.axis_index("cont")
    x, core, z, y = b // 2, b % 2, c // 4, c % 4

    def cont_peer(k):
        i, j = k // 4, k % 4
        dz = 4 + (1 - 2 * (i % 2)) * ((i + 1) // 2)
        dy = 2 + (1 - 2 * (j % 2)) * ((j + 1) // 2)
        return ((z + dz) % 8) * 4 + (y + dy) % 4

    def moved(dz, dy):
        return ((z + dz) % 8) * 4 + (y + dy) % 4

    def antipode(p):
        return ((p // 4 + 4) % 8) * 4 + (p % 4 + 2) % 4

    body_peers = [
        ((x + dx) % 4) * 2 + (core + dc) % 2
        for dx, dc in ((2, 1), (2, 0), (1, 1), (3, 1), (1, 0), (3, 0), (0, 1))
    ]

    def over_cont(go):
        def one(k, carry):
            go(cont_peer(k))
            return carry

        lax.fori_loop(0, 31, one, 0)

    def send_body(src, dst, ssem, rsem):
        for p in body_peers:
            pltpu.make_async_remote_copy(
                src_ref=src, dst_ref=dst, send_sem=ssem, recv_sem=rsem,
                device_id={"body": p}, device_id_type=MESH,
            ).start()

    def drain(ref, sem):
        pltpu.make_async_copy(ref, ref, sem).wait()

    bar = pltpu.get_barrier_semaphore()
    over_cont(lambda p: pl.semaphore_signal(bar, inc=1, device_id={"cont": p}, device_id_type=MESH))
    for p in body_peers:
        pl.semaphore_signal(bar, inc=1, device_id={"body": p}, device_id_type=MESH)

    pairs = (
        (warm_in, warm), (live_in, livev), (row_in, rowv), (col_in, colv), (step_in, step),
        (bias_in, bias), (fric_in, fric), (free_in, free), (mass_in, mass),
    )
    small = [pltpu.make_async_copy(s, d, in_sem.at[n]) for n, (s, d) in enumerate(pairs)]
    for cp in small:
        cp.start()
    blocks = [
        pltpu.make_async_copy(jac_in.at[pl.ds(n * 6, 6)], jac.at[pl.ds(n * 6, 6)], jac_sem.at[n])
        for n in range(5)
    ]
    for cp in blocks:
        cp.start()
    for cp in small[:2]:
        cp.wait()

    lane16 = iota((16, 128), 1)
    low16 = lane16 < 64
    lane8 = iota((8, 128), 1)
    low8 = lane8 < 64

    def rows_of(get):
        parts = [get(p).astype(F32) for p in range(5)]
        return jnp.concatenate(parts + [jnp.zeros((3, 128), F32)], axis=0)

    def planes(ref):
        w0, w1, w2 = [rows_of(lambda p, i=i: ref[i, 0:1, p * 128:(p + 1) * 128]) for i in range(3)]
        even = jnp.where(low8, w0, half_turn(w1))
        odd = jnp.where(low8, half_turn(w0), w1)
        return jnp.concatenate([even, odd], 0), jnp.concatenate([w2, half_turn(w2)], 0)

    def high_plane(ref):
        f = rows_of(lambda p: ref[0:1, p * 128:(p + 1) * 128])
        return jnp.concatenate([half_turn(f), f], 0)

    sub10 = iota((16, 10), 0)
    block_of_row = 2 * (sub10 & 7) + (sub10 >> 3)
    live_row = jnp.sum(
        jnp.where(iota((16, 10), 1) == block_of_row, livev[...].astype(F32), 0.0), axis=1, keepdims=True
    )
    active = (lane16 & 63).astype(F32) < live_row
    wa, wb = planes(warm)
    wa, wb = jnp.where(active, wa, 0.0), jnp.where(active & low16, wb, 0.0)
    tab_send[0] = wa.astype(BF16)
    tab_send[1] = wb.astype(BF16)
    pl.semaphore_wait(bar, 38)
    send_body(tab_send, tab_recv.at[b], tab_s, tab_r)
    tab_recv[b] = tab_send[...]

    for cp in small[2:]:
        cp.wait()
    sa, sb = planes(step)
    con_send[0] = wa
    con_send[1] = jnp.where(low16, wb, jnp.where(active, high_plane(fric), -1.0))
    con_send[2] = sa
    con_send[3] = jnp.where(low16, sb, high_plane(bias))

    ids[0:1, :] = jnp.where(iota((1, 128), 1) < 32, 9999, 0)
    ids[1:2, :] = jnp.where(iota((1, 128), 1) < 32, 10000, 0)
    ids[0:1, 0:SLOTS] = rowv[...]
    ids[1:2, 0:SLOTS] = colv[...]
    lane1 = iota((1, 128), 1)
    row_l = ids[0:1, :]
    dev = (row_l * 52429) >> 19
    kk = row_l - 10 * dev
    place_l = jnp.where(
        lane1 < SLOTS, dev * 16 + (kk & 1) * 8 + (kk >> 1), jnp.where(lane1 < 32, 9999, 0)
    ).astype(F32)
    col_l = ids[1:2, :]
    owner_i = (col_l * 52429) >> 18
    within_l = (col_l - 5 * owner_i).astype(F32)
    owner_l = owner_i.astype(F32)

    sub32, lane32 = iota((32, 128), 0), iota((32, 128), 1)

    def down(v):
        return jnp.sum(jnp.where(sub32 == lane32, jnp.broadcast_to(v, (32, 128)), 0.0), axis=1, keepdims=True)

    place_s, owner_s, within_s = down(place_l), down(owner_l), down(within_l)
    rank_l = jnp.sum(
        jnp.where((owner_s == owner_l) & (sub32 < lane32) & (lane32 < 32), 1.0, 0.0), axis=0, keepdims=True
    )
    place8 = jnp.broadcast_to(place_l, (8, 128))
    con_send[4, 0:8, :] = pltpu.roll(jnp.where(lane8 < 16, place8, 0.0), b * 16, axis=1)
    con_send[4, 8:16, :] = pltpu.roll(jnp.where((lane8 >= 16) & (lane8 < 32), place8, 0.0), (b * 16 + 112) % 128, axis=1)

    def four_times(v):
        v = jnp.broadcast_to(v, (8, 128))
        v = v + pltpu.roll(v, 32, axis=1)
        return (v + pltpu.roll(v, 64, axis=1))[0:1]

    owner4, rank4 = four_times(owner_l), four_times(rank_l)
    sub = iota((320, 1), 0)
    o_row = jnp.where(sub < 256, sub >> 3, jnp.where(sub < 288, sub - 256, (sub - 288) ^ 18))
    m_row = jnp.where(sub < 256, sub & 7, 8)
    r_row = jnp.where(m_row < 3, 0, jnp.where(m_row < 6, 1, 2))
    c_row = m_row - 3 * r_row
    hit = (owner4 == o_row.astype(F32)) & (rank4 == r_row.astype(F32))
    for tile in range(2):
        q = (iota((1, 128), 1) >> 5) + 4 * tile
        cq = jnp.where(q < 3, q, jnp.where(q < 6, q - 3, -1))
        pick[:, tile * 128:(tile + 1) * 128] = jnp.where(hit & (cq == c_row), 1.0, 0.0).astype(BF16)
    sub96 = iota((96, 1), 0)
    c96 = (sub96 >> 5).astype(F32)
    place = jnp.full((32, 1), -1000.0, F32)
    for k, (dz, dy) in enumerate(NEAR + ((0, 0),)):
        near = moved(8 - dz, 4 - dy)
        place = jnp.where(owner_s == near.astype(F32), float(k * 32), place)
        place = jnp.where(owner_s == antipode(near).astype(F32), float(k * 32 + 16), place)
    target96 = jnp.concatenate([place + within_s] * 3, axis=0) + 5 * c96
    meta_send[...] = jnp.where(lane1 < SLOTS, owner_l * 16 + rank_l * 5 + within_l, 9999.0)
    gather_one[...] = jnp.where(iota((96, 512), 1).astype(F32) == target96, 1.0, 0.0).astype(BF16)
    own_s = (b * 16 + iota((16, 1), 0)).astype(F32)
    place48 = jnp.concatenate([place_s, own_s], axis=0)
    slot_one[...] = jnp.where(iota((48, 128), 1).astype(F32) == place48, 1.0, 0.0).astype(BF16)
    for n, src in enumerate((free, mass)):
        rows = [src[w, 0:1, i * 128:(i + 1) * 128] for i in range(3) for w in range(5)]
        home[0, n] = jnp.concatenate(rows + [jnp.zeros((1, 128), F32)], axis=0)

    con_recv[b] = con_send[...]

    pltpu.make_async_remote_copy(
        src_ref=home.at[0], dst_ref=home.at[1], send_sem=home_s, recv_sem=home_r,
        device_id={"cont": antipode(c)}, device_id_type=MESH,
    ).start()

    def send_meta(p):
        pltpu.make_async_remote_copy(
            src_ref=meta_send, dst_ref=meta_recv.at[c], send_sem=meta_s, recv_sem=meta_r,
            device_id={"cont": p}, device_id_type=MESH,
        ).start()

    over_cont(send_meta)
    meta_recv[c] = meta_send[...]

    drain(tab_recv.at[pl.ds(0, 7)], tab_r)
    imp_a[...] = mm(slot_one[...], tab_recv[:, 0].reshape(128, 128))
    imp_b[...] = mm(slot_one[...], tab_recv[:, 1].reshape(128, 128))
    for cp in blocks:
        cp.wait()

    low32 = lane32 < 64

    def forces():
        ya, yb = imp_a[0:32, :], imp_b[0:32, :]
        turned = half_turn(ya)
        pattern = jnp.concatenate(
            [ya, jnp.where(low32, yb, turned), jnp.where(low32, turned, half_turn(yb))], axis=1
        ).astype(BF16)
        halves = []
        row = iota((16, 768), 0)
        lane = iota((16, 768), 1) // 192
        for h in range(2):
            rep = jnp.concatenate([pattern[16 * h:16 * h + 16]] * 2, axis=1)
            acc = jnp.zeros((16, 384), F32)
            for g in range(0, 16, 4):
                s = 16 * h + g
                n = min(4, SLOTS - s)
                lhs = jnp.where(lane + g == row, rep, jnp.zeros_like(rep))[:, :n * 192]
                acc = acc + mm(lhs, jac[s:s + n].reshape(n * 192, 384))
            halves.append(acc)
        return jnp.concatenate(halves, axis=0)

    def locals_of(v, h):
        row = iota((16, 768), 0) // 2
        lane = iota((16, 768), 1) // 384
        rep = jnp.concatenate([v[16 * h:16 * h + 16]] * 2, axis=1)
        acc = jnp.zeros((16, 384), F32)
        for g in range(0, 8, 2):
            p = 8 * h + g
            n = min(2, SLOTS // 2 - p)
            lhs = jnp.where(lane + g == row, rep, jnp.zeros_like(rep))[:, :n * 384]
            acc = acc + mm(lhs, jact[p:p + n].reshape(n * 384, 384))
        return acc

    def sweep(t, carry):
        sf = forces()
        most = jnp.max(jnp.abs(sf), axis=0, keepdims=True)
        most = jnp.maximum(jnp.maximum(most[:, 0:128], most[:, 128:256]), most[:, 256:384])
        most = jnp.max(most, axis=1, keepdims=True)
        power = jnp.floor(jnp.log2(jnp.maximum(jnp.broadcast_to(most, (1, 128)), 1e-30))) + 1.0
        scale = jnp.exp2(15.0 - power)
        code = jnp.clip(jnp.round(sf * jnp.concatenate([scale] * 3, axis=1)), -32767.0, 32767.0)
        hi, mid = split(code)
        stacked = jnp.concatenate(
            [part[:, n * 128:(n + 1) * 128] for part in (hi, mid) for n in range(3)], axis=0
        )
        packed = mm(pick[:, 0:192], stacked).astype(I32)
        other = jnp.concatenate([packed[8 * (o ^ 18):8 * (o ^ 18) + 8] for o in range(32)], axis=0)
        force_send[t, :, 0:8, :] = (packed[0:256] * 65536 + other).reshape(32, 8, 128)
        force_send[t, :, 8:9, :] = (packed[256:288] * 65536 + packed[288:320]).reshape(32, 1, 128)
        force_send[t, :, 9:10, :] = jnp.broadcast_to(power.astype(I32).reshape(1, 1, 128), (32, 1, 128))

        def send_force(p):
            pltpu.make_async_remote_copy(
                src_ref=force_send.at[t, p], dst_ref=force_recv.at[t, c], send_sem=force_s.at[t],
                recv_sem=force_r.at[t], device_id={"cont": p}, device_id_type=MESH,
            ).start()

        over_cont(send_force)
        force_recv[t, c] = force_send[t, c]

        @pl.when(t == 0)
        def _():
            send_body(con_send, con_recv.at[b], con_s, con_r)
            drain(home.at[1], home_r)
            drain(meta_recv.at[pl.ds(0, 31)], meta_r)
            codes = meta_recv[...].reshape(32, 128)
            line = iota((32, 8, 128), 1)
            lane288 = iota((288, 128), 1).astype(F32)
            sub288 = iota((288, 128), 0)
            m288 = jnp.where(sub288 < 256, sub288 & 7, 8)
            col288 = (m288 - 3 * jnp.where(m288 < 3, 0, jnp.where(m288 < 6, 1, 2))).astype(F32)
            for role, h in enumerate((c, antipode(c))):
                rel = codes - (16 * h).astype(F32)
                found = []
                for r in range(3):
                    fits = (rel >= 5 * r) & (rel < 5 * r + 5)
                    one = jnp.sum(jnp.where(fits, rel - (5 * r - 1), 0.0), axis=1, keepdims=True)
                    found.append(jnp.broadcast_to(one, (32, 128)))
                wide = [jnp.broadcast_to(f.reshape(32, 1, 128), (32, 8, 128)) for f in found]
                rows = jnp.where(line < 3, wide[0], jnp.where(line < 6, wide[1], wide[2])).reshape(256, 128)
                rows = jnp.concatenate([rows, found[2]], axis=0)
                hits = (rows > 0.0) & (lane288 == rows - 1.0 + 5 * col288)
                meta = jnp.concatenate([jnp.where(hits, 1.0, 0.0), jnp.zeros((96, 128), F32)], axis=0)
                owner_one[role] = jnp.transpose(meta)[0:16].astype(BF16)
            for p in range(SLOTS // 2):
                jact[p] = jnp.transpose(jac[2 * p:2 * p + 2].reshape(384, 384))
            drain(con_recv.at[pl.ds(0, 7)], con_r)
            for h in range(2):
                got_ids = con_recv[0, 4, 8 * h:8 * h + 1, :]
                for d in range(1, 8):
                    got_ids = got_ids + con_recv[d, 4, 8 * h:8 * h + 1, :]
                row_one[:, h * 128:(h + 1) * 128] = jnp.where(got_ids == place48, 1.0, 0.0).astype(BF16)
            low48 = iota((48, 128), 1) < 64

            def exact(n):
                plane = con_recv[:, n].reshape(128, 128)
                p0, p1 = split(plane)
                p2 = (plane - p0.astype(F32) - p1.astype(F32)).astype(BF16)
                return mm(slot_one[...], p0) + (mm(slot_one[...], p1) + mm(slot_one[...], p2))

            imp_a[...] = exact(0)
            both = exact(1)
            imp_b[...] = jnp.where(low48, both, 0.0)
            fric48[...] = jnp.where(low48, half_turn(both), both)
            step_a[...] = exact(2)
            both = exact(3)
            step_b[...] = both
            shift48[...] = jnp.where(low48, half_turn(both), 0.0)

        drain(force_recv.at[t, pl.ds(0, 31)], force_r.at[t])
        word = jnp.concatenate(
            [force_recv[t, :, 0:8, :].reshape(256, 128), force_recv[t, :, 8:9, :].reshape(32, 128)], axis=0
        )
        unit = jnp.exp2(force_recv[t, :, 9:10, :].reshape(32, 128).astype(F32) - 15.0)
        units = jnp.concatenate(
            [jnp.broadcast_to(unit.reshape(32, 1, 128), (32, 8, 128)).reshape(256, 128), unit], axis=0
        )
        upper = (word + 32768) >> 16
        both_homes = []
        for role, value in enumerate((upper, word - (upper << 16))):
            parts = jnp.concatenate(split(value.astype(F32) * units), axis=1)
            force = mm(owner_one[role, :, 0:288], parts)
            force = force[:, 0:128] + force[:, 128:256]
            both_homes.append(home[role, 0] + home[role, 1] * force)
        velocity = both_homes[0]

        @pl.when(t == SWEEPS)
        def _():
            for n in range(3):
                for w in range(5):
                    i, p = divmod(w * 3 + n, 5)
                    out[3 + i, 0:1, p * 128:(p + 1) * 128] = velocity[n * 5 + w:n * 5 + w + 1]

        @pl.when(t < SWEEPS)
        def _():
            vel_send[t] = jnp.concatenate(both_homes, axis=0).astype(BF16)
            for k, (dz, dy) in enumerate(NEAR):
                pltpu.make_async_remote_copy(
                    src_ref=vel_send.at[t], dst_ref=vel_recv.at[t, k], send_sem=vel_s.at[t],
                    recv_sem=vel_r.at[t], device_id={"cont": moved(dz, dy)}, device_id_type=MESH,
                ).start()
            vel_recv[t, 15] = vel_send[t]
            drain(vel_recv.at[t, pl.ds(0, 15)], vel_r.at[t])
            vs = mm(gather_one[...], vel_recv[t].reshape(512, 128)).astype(BF16)
            v = jnp.concatenate([vs[0:32], vs[32:64], vs[64:96]], axis=1)
            even = (iota((16, 128), 0) & 1) == 0
            for h in range(2):
                loc = locals_of(v, h)
                l0, l1, l2 = loc[:, 0:128], loc[:, 128:256], loc[:, 256:384]
                t2 = half_turn(l2)
                la = jnp.where(even, l0, jnp.where(low16, half_turn(l1), t2))
                lb = jnp.where(even, l1, t2)
                ahi, amid = split(la)
                bhi = lb.astype(BF16).astype(F32)
                loc_send[t, h, 0] = ahi
                loc_send[t, h, 1] = amid
                loc_send[t, h, 2] = jnp.where(low16, bhi, half_turn(lb - bhi)).astype(BF16)
                send_body(loc_send.at[t, h], loc_recv.at[t, h, b], loc_s.at[t, h], loc_r.at[t, h])
                loc_recv[t, h, b] = loc_send[t, h]
            lv = jnp.zeros((48, 384), F32)
            for h in range(2):
                drain(loc_recv.at[t, h, pl.ds(0, 7)], loc_r.at[t, h])
                got_loc = jnp.concatenate([loc_recv[t, h, :, n].reshape(128, 128) for n in range(3)], axis=1)
                lv = lv + mm(row_one[:, h * 128:(h + 1) * 128], got_loc)
            lva = lv[:, 0:128] + lv[:, 128:256]
            lvb = lv[:, 256:384] + half_turn(lv[:, 256:384])
            low = iota((48, 128), 1) < 64
            fr = fric48[...]
            ta = imp_a[...] - step_a[...] * (lva + shift48[...])
            tb = imp_b[...] - step_b[...] * lvb
            normal = jnp.where(low, jnp.maximum(ta, 0.0), 0.0)
            lim_a = fr * half_turn(normal)
            lim_b = fr * normal
            live = fr >= 0.0
            new_a = jnp.where(low, normal, jnp.clip(ta, -lim_a, lim_a))
            imp_a[...] = jnp.where(live, new_a, 0.0)
            imp_b[...] = jnp.where(live & low, jnp.clip(tb, -lim_b, lim_b), 0.0)

        return carry

    lax.fori_loop(0, SWEEPS + 1, sweep, 0)

    own_a, own_b = imp_a[32:48, :], imp_b[32:48, :]
    ae, ao, be, bo = own_a[0:8], own_a[8:16], own_b[0:8], own_b[8:16]
    outs = (
        jnp.where(low8, ae, half_turn(ao)),
        jnp.where(low8, half_turn(ae), ao),
        jnp.where(low8, be, half_turn(bo)),
    )
    for i in range(3):
        for p in range(5):
            out[i, 0:1, p * 128:(p + 1) * 128] = outs[i][p:p + 1]

    drain(tab_recv.at[pl.ds(0, 7)], tab_s)
    drain(con_recv.at[pl.ds(0, 7)], con_s)
    drain(meta_recv.at[pl.ds(0, 31)], meta_s)
    drain(home.at[1], home_s)
    for t in range(SWEEPS + 1):
        drain(force_recv.at[t, pl.ds(0, 31)], force_s.at[t])
        if t < SWEEPS:
            drain(vel_recv.at[t, pl.ds(0, 15)], vel_s.at[t])
            for h in range(2):
                drain(loc_recv.at[t, h, pl.ds(0, 7)], loc_s.at[t, h])


def shards(jacobian, row, col, live, warm, step, bias, fric, free, mass):
    dma = pltpu.SemaphoreType.DMA
    passes = SWEEPS + 1
    hbm = pl.BlockSpec(memory_space=pl.ANY)
    vmem = pl.BlockSpec(memory_space=pltpu.VMEM)
    out = pl.pallas_call(
        kernel,
        out_shape=jax.ShapeDtypeStruct((6, 1, 640), F32),
        in_specs=[hbm] * 10,
        out_specs=vmem,
        scratch_shapes=[
            pltpu.VMEM((SLOTS, 3, 64, 384), BF16),
            pltpu.VMEM((1, SLOTS), I32),
            pltpu.VMEM((1, SLOTS), I32),
            pltpu.VMEM((1, 10), I32),
            pltpu.VMEM((3, 1, 640), F32),
            pltpu.VMEM((3, 1, 640), F32),
            pltpu.VMEM((1, 640), F32),
            pltpu.VMEM((1, 640), F32),
            pltpu.VMEM((5, 1, 384), F32),
            pltpu.VMEM((5, 1, 384), F32),
            pltpu.VMEM((SLOTS // 2, 384, 384), BF16),
            pltpu.VMEM((8, 128), I32),
            pltpu.VMEM((320, 256), BF16),
            pltpu.VMEM((2, 16, 384), BF16),
            pltpu.VMEM((48, 128), BF16),
            pltpu.VMEM((48, 256), BF16),
            pltpu.VMEM((96, 512), BF16),
            pltpu.VMEM((48, 128), F32),
            pltpu.VMEM((48, 128), F32),
            pltpu.VMEM((48, 128), F32),
            pltpu.VMEM((48, 128), F32),
            pltpu.VMEM((48, 128), F32),
            pltpu.VMEM((48, 128), F32),
            pltpu.VMEM((2, 2, 16, 128), F32),
            pltpu.VMEM((2, 16, 128), BF16),
            pltpu.VMEM((8, 2, 16, 128), BF16),
            pltpu.VMEM((5, 16, 128), F32),
            pltpu.VMEM((8, 5, 16, 128), F32),
            pltpu.VMEM((1, 128), F32),
            pltpu.VMEM((32, 1, 128), F32),
            pltpu.VMEM((passes, 32, 10, 128), I32),
            pltpu.VMEM((passes, 32, 10, 128), I32),
            pltpu.VMEM((SWEEPS, 32, 128), BF16),
            pltpu.VMEM((SWEEPS, 16, 32, 128), BF16),
            pltpu.VMEM((SWEEPS, 2, 3, 16, 128), BF16),
            pltpu.VMEM((SWEEPS, 2, 8, 3, 16, 128), BF16),
            dma((5,)), dma((9,)), dma, dma, dma, dma, dma, dma, dma, dma,
            dma((passes,)), dma((passes,)), dma((SWEEPS,)), dma((SWEEPS,)), dma((SWEEPS, 2)), dma((SWEEPS, 2)),
        ],
        compiler_params=pltpu.CompilerParams(
            collective_id=0, has_side_effects=True, vmem_limit_bytes=63 << 20
        ),
        name="sweeps",
    )(jacobian.reshape(jacobian.shape[1:]), row, col, live, warm, step, bias, fric,
      free.transpose(1, 0, 2), mass.transpose(1, 0, 2))
    return out[0:3], out[3:6].reshape(5, 1, 384).transpose(1, 0, 2)


def solution(mesh):
    placed = (
        P("body", "cont", None, None, None),
        P("body", "cont"),
        P("body", "cont"),
        P("cont", "body"),
        P(None, "cont", "body"),
        P(None, "cont", "body"),
        P("cont", "body"),
        P("cont", "body"),
        P("body", "cont", None),
        P("body", "cont", None),
    )
    return jax.shard_map(
        shards,
        mesh=mesh,
        in_specs=placed,
        out_specs=(P(None, "cont", "body"), P("body", "cont", None)),
        check_vma=False,
    )
```

time: 92.5 us -> 82.3 us (0.89)
  local copies, waits for them, and re-layouts: 9.56 us -> 1.32 us
  Pallas kernels: 82 us -> 80.1 us
    unnamed x19 -> x0, local copies, waits for them, and re-layouts: 8.96 us -> none
    pallas_call x1, Pallas kernels: 82 us -> 80.1 us  [shards(): pl.pallas_call(kernel, out_shape=jax.ShapeDtypeStruct((6, 1, 640), F32),...]
    slice x0 -> x1, local copies, waits for them, and re-layouts: none -> 1.32 us  [shards(): return (out[0:3], out[3:6].reshape(5, 1, 384).transpose(1, 0, 2))]
where the time goes in v2:
time: 82.3 us; the launch traced here: 82 us
  Pallas kernels  80.1 us (97%)
  local copies, waits for them, and re-layouts  1.32 us (2%)
    pallas_call x1, Pallas kernels, shards(): pl.pallas_call(kernel, out_shape=jax.ShapeDtypeStruct((6, 1, 640), F32),...  80.1 us

profile of v2, /device:TPU:1, one launch (start us, length us, event | category | flops | bytes accessed | tf_op | source)
XLA Modules:
  0.0 82.0 jit_solution(7604696492481968030)
XLA Ops:
  0.6 80.1 %sweeps.1 = f32[6,1,640]{2,1,0:T(1,128)} custom-call(bf16[30,3,64,384]{3,2,1,0:T(8,128)(2,1)} %bitcast.4, s32[1,30]{1,0:T(1,128)} %row_in.1, s32[1,30]{1,0:T(1,128)} %col_in.1, s32[1,10]{1,0:T(1,128)} %live_in.1, f32[3,1,640]{2,1,0:T(1,128)} %warm_in.1, f32[3,1,640]{2,1,0:T(1,128)} %step_in.1, f32[1,640]{1,0:T(1,128)} %bias_in.1, f32[1,640]{1,0:T(1,128)} %fric_in.1, ...), custom_call_target="tpu_custom_call" | custom-call | tf_op jit(solution)/shard_map/sweeps/pallas_call | solution.py:441
  80.7 1.3 %fusion = (f32[3,1,640]{2,1,0:T(1,128)}, f32[3,1,640]{2,1,0:T(1,128)}) fusion(f32[6,1,640]{2,1,0:T(1,128)} %sweeps.1), kind=kLoop, calls=%fused_computation | loop fusion | bytes 30720 | tf_op jit(solution)/shard_map/slice | solution.py:492

commit v3 on v2

--- a/solution.py
+++ b/solution.py
@@ -484,11 +484,16 @@
             dma((passes,)), dma((passes,)), dma((SWEEPS,)), dma((SWEEPS,)), dma((SWEEPS, 2)), dma((SWEEPS, 2)),
         ],
         compiler_params=pltpu.CompilerParams(
-            collective_id=0, has_side_effects=True, vmem_limit_bytes=63 << 20
+            collective_id=0, has_side_effects=True, vmem_limit_bytes=32 << 20
         ),
         name="sweeps",
-    )(jacobian.reshape(jacobian.shape[1:]), row, col, live, warm, step, bias, fric,
-      free.transpose(1, 0, 2), mass.transpose(1, 0, 2))
+    )(*[
+        pltpu.with_memory_space_constraint(v, pltpu.HBM)
+        for v in (
+            jacobian.reshape(jacobian.shape[1:]), row, col, live, warm, step, bias, fric,
+            free.transpose(1, 0, 2), mass.transpose(1, 0, 2),
+        )
+    ])
     return out[0:3], out[3:6].reshape(5, 1, 384).transpose(1, 0, 2)
 
 

time: 82.3 us -> 80.9 us (0.983)
  no operation moved by 1% of the time
where the time goes in v3:
time: 80.9 us; the launch traced here: 80.7 us
  Pallas kernels  79.5 us (98%)
    pallas_call x1, Pallas kernels, shards(): pl.pallas_call(kernel, out_shape=jax.ShapeDtypeStruct((6, 1, 640), F32),...  79.5 us

profile of v3, /device:TPU:1, one launch (start us, length us, event | category | flops | bytes accessed | tf_op | source)
XLA Modules:
  0.0 80.7 jit_solution(8056981660344650840)
XLA Ops:
  0.6 79.5 %sweeps.1 = f32[6,1,640]{2,1,0:T(1,128)S(1)} custom-call(bf16[30,3,64,384]{3,2,1,0:T(8,128)(2,1)} %bitcast.4, s32[1,30]{1,0:T(1,128)} %row_in.1, s32[1,30]{1,0:T(1,128)} %col_in.1, s32[1,10]{1,0:T(1,128)} %live_in.1, f32[3,1,640]{2,1,0:T(1,128)} %warm_in.1, f32[3,1,640]{2,1,0:T(1,128)} %step_in.1, f32[1,640]{1,0:T(1,128)} %bias_in.1, f32[1,640]{1,0:T(1,128)} %fric_in.1, ...), custom_call_target="tpu_custom_call" | custom-call | tf_op jit(solution)/shard_map/sweeps/pallas_call | solution.py:441
  80.1 0.6 fusion

commit v4 on v3

--- a/solution.py
+++ b/solution.py
@@ -65,11 +65,8 @@
     ]
 
     def over_cont(go):
-        def one(k, carry):
+        for k in range(31):
             go(cont_peer(k))
-            return carry
-
-        lax.fori_loop(0, 31, one, 0)
 
     def send_body(src, dst, ssem, rsem):
         for p in body_peers:
@@ -336,6 +333,29 @@
             both = exact(3)
             step_b[...] = both
             shift48[...] = jnp.where(low48, half_turn(both), 0.0)
+
+        @pl.when(t == SWEEPS)
+        def _():
+            own_a, own_b = imp_a[32:48, :], imp_b[32:48, :]
+            ae, ao, be, bo = own_a[0:8], own_a[8:16], own_b[0:8], own_b[8:16]
+            outs = (
+                jnp.where(low8, ae, half_turn(ao)),
+                jnp.where(low8, half_turn(ae), ao),
+                jnp.where(low8, be, half_turn(bo)),
+            )
+            for i in range(3):
+                for p in range(5):
+                    out[i, 0:1, p * 128:(p + 1) * 128] = outs[i][p:p + 1]
+
+            drain(tab_recv.at[pl.ds(0, 7)], tab_s)
+            drain(con_recv.at[pl.ds(0, 7)], con_s)
+            drain(meta_recv.at[pl.ds(0, 31)], meta_s)
+            drain(home.at[1], home_s)
+            for n in range(SWEEPS):
+                drain(force_recv.at[n, pl.ds(0, 31)], force_s.at[n])
+                drain(vel_recv.at[n, pl.ds(0, 15)], vel_s.at[n])
+                for h in range(2):
+                    drain(loc_recv.at[n, h, pl.ds(0, 7)], loc_s.at[n, h])
 
         drain(force_recv.at[t, pl.ds(0, 31)], force_r.at[t])
         word = jnp.concatenate(
@@ -410,27 +430,7 @@
 
     lax.fori_loop(0, SWEEPS + 1, sweep, 0)
 
-    own_a, own_b = imp_a[32:48, :], imp_b[32:48, :]
-    ae, ao, be, bo = own_a[0:8], own_a[8:16], own_b[0:8], own_b[8:16]
-    outs = (
-        jnp.where(low8, ae, half_turn(ao)),
-        jnp.where(low8, half_turn(ae), ao),
-        jnp.where(low8, be, half_turn(bo)),
-    )
-    for i in range(3):
-        for p in range(5):
-            out[i, 0:1, p * 128:(p + 1) * 128] = outs[i][p:p + 1]
-
-    drain(tab_recv.at[pl.ds(0, 7)], tab_s)
-    drain(con_recv.at[pl.ds(0, 7)], con_s)
-    drain(meta_recv.at[pl.ds(0, 31)], meta_s)
-    drain(home.at[1], home_s)
-    for t in range(SWEEPS + 1):
-        drain(force_recv.at[t, pl.ds(0, 31)], force_s.at[t])
-        if t < SWEEPS:
-            drain(vel_recv.at[t, pl.ds(0, 15)], vel_s.at[t])
-            for h in range(2):
-                drain(loc_recv.at[t, h, pl.ds(0, 7)], loc_s.at[t, h])
+    drain(force_recv.at[SWEEPS, pl.ds(0, 31)], force_s.at[SWEEPS])
 
 
 def shards(jacobian, row, col, live, warm, step, bias, fric, free, mass):

time: 80.9 us -> 79.3 us (0.980)
  Pallas kernels: 79.5 us -> 77.9 us
    pallas_call x1, Pallas kernels: 79.5 us -> 77.9 us  [shards(): pl.pallas_call(kernel, out_shape=jax.ShapeDtypeStruct((6, 1, 640), F32),...]
where the time goes in v4:
time: 79.3 us; the launch traced here: 79.2 us
  Pallas kernels  77.9 us (98%)
    pallas_call x1, Pallas kernels, shards(): pl.pallas_call(kernel, out_shape=jax.ShapeDtypeStruct((6, 1, 640), F32),...  77.9 us

profile of v4, /device:TPU:1, one launch (start us, length us, event | category | flops | bytes accessed | tf_op | source)
XLA Modules:
  0.0 79.2 jit_solution(2085702675896888282)
XLA Ops:
  0.6 77.9 %sweeps.1 = f32[6,1,640]{2,1,0:T(1,128)S(1)} custom-call(bf16[30,3,64,384]{3,2,1,0:T(8,128)(2,1)} %bitcast.4, s32[1,30]{1,0:T(1,128)} %row_in.1, s32[1,30]{1,0:T(1,128)} %col_in.1, s32[1,10]{1,0:T(1,128)} %live_in.1, f32[3,1,640]{2,1,0:T(1,128)} %warm_in.1, f32[3,1,640]{2,1,0:T(1,128)} %step_in.1, f32[1,640]{1,0:T(1,128)} %bias_in.1, f32[1,640]{1,0:T(1,128)} %fric_in.1, ...), custom_call_target="tpu_custom_call" | custom-call | tf_op jit(solution)/shard_map/sweeps/pallas_call | solution.py:441
  78.6 0.6 fusion

commit v5 on v4

--- a/solution.py
+++ b/solution.py
@@ -12,6 +12,10 @@
     (1, 2), (7, 2), (2, 1), (6, 1), (2, 0), (6, 0), (1, 1), (1, 3), (7, 1), (7, 3), (0, 2),
     (1, 0), (7, 0), (0, 1), (0, 3),
 )
+FAR_FIRST = tuple(sorted(
+    ((dz, dy) for dz in (4, 3, 5, 2, 6, 1, 7, 0) for dy in (2, 1, 3, 0) if (dz, dy) != (0, 0)),
+    key=lambda step: -min(step[0], 8 - step[0]) - min(step[1], 4 - step[1]),
+))
 F32, BF16, I32 = jnp.float32, jnp.bfloat16, jnp.int32
 
 
@@ -47,12 +51,6 @@
     b, c = lax.axis_index("body"), lax.axis_index("cont")
     x, core, z, y = b // 2, b % 2, c // 4, c % 4
 
-    def cont_peer(k):
-        i, j = k // 4, k % 4
-        dz = 4 + (1 - 2 * (i % 2)) * ((i + 1) // 2)
-        dy = 2 + (1 - 2 * (j % 2)) * ((j + 1) // 2)
-        return ((z + dz) % 8) * 4 + (y + dy) % 4
-
     def moved(dz, dy):
         return ((z + dz) % 8) * 4 + (y + dy) % 4
 
@@ -65,8 +63,8 @@
     ]
 
     def over_cont(go):
-        for k in range(31):
-            go(cont_peer(k))
+        for dz, dy in FAR_FIRST:
+            go(moved(dz, dy))
 
     def send_body(src, dst, ssem, rsem):
         for p in body_peers:

time: 79.3 us -> 78.9 us (level)
  no operation moved by 1% of the time
where the time goes in v5:
time: 78.9 us; the launch traced here: 78.8 us
  Pallas kernels  77.5 us (98%)
    pallas_call x1, Pallas kernels, shards(): pl.pallas_call(kernel, out_shape=jax.ShapeDtypeStruct((6, 1, 640), F32),...  77.5 us

profile of v5, /device:TPU:1, one launch (start us, length us, event | category | flops | bytes accessed | tf_op | source)
XLA Modules:
  0.0 78.8 jit_solution(4099341459195113087)
XLA Ops:
  0.6 77.5 %sweeps.1 = f32[6,1,640]{2,1,0:T(1,128)S(1)} custom-call(bf16[30,3,64,384]{3,2,1,0:T(8,128)(2,1)} %bitcast.4, s32[1,30]{1,0:T(1,128)} %row_in.1, s32[1,30]{1,0:T(1,128)} %col_in.1, s32[1,10]{1,0:T(1,128)} %live_in.1, f32[3,1,640]{2,1,0:T(1,128)} %warm_in.1, f32[3,1,640]{2,1,0:T(1,128)} %step_in.1, f32[1,640]{1,0:T(1,128)} %bias_in.1, f32[1,640]{1,0:T(1,128)} %fric_in.1, ...), custom_call_target="tpu_custom_call" | custom-call | tf_op jit(solution)/shard_map/sweeps/pallas_call | solution.py:439
  78.1 0.6 fusion
